TPU v7x, 32 devices: a whole 2x2x4 slice. The times are simulated.
32 devices in a mesh: grp: 2 (over y), seq: 4 (over z), col: 4 (over x, core).
Axes of the slice: x: 2, y: 2, z: 4, core: 2. Of those that a mesh axis runs over, the one named last changes fastest.
Arguments:
- tokens: bfloat16 [4096, 4608], P(('grp', 'seq'), 'col'), parts along dimension 0, may hold values from -14 to 14
- norm_gain: float32 [4608], replicated, may hold values from 0.5 to 1.5
- query_weight: bfloat16 [4608, 2048], P('seq', 'col'), may hold values from -1 to 1
- key_weight: bfloat16 [4608, 1024], P('seq', 'col'), may hold values from -1 to 1
- value_weight: bfloat16 [4608, 1024], P('seq', 'col'), may hold values from -0.09375 to 0.09375
- out_weight: bfloat16 [2048, 4608], P('seq', 'col'), may hold values from -1 to 1
- positions: int32 [4096], P(('grp', 'seq')), parts along dimension 0, may hold values from 0 to 2047, as said below
Outputs:
- block_out: bfloat16 [4096, 4608], P(('grp', 'seq'), 'col'), parts along dimension 0
There are 2 independent parts, one for each index of `grp`. A program takes and returns all parts, laid end to end along the dimension named above; an argument that names none is the same for every part. Nothing has to cross between parts.
Inputs may be any that keep to these rules, and one draw needn't show every extreme that they name: Within a document positions rise by one from token to token. Exactly one document starts inside the slab, at a token of its middle half, where positions restart at 0; the document before it ends at position 2047.
All inputs are finite; a program needn't handle non-finite values.
Results may differ from a plain program's by a relative error of at most 0.012.
The roundings to bfloat16 on the way count: a program that leaves them out, or rounds other values in their place, can miss the bound.
Values may be sent and summed in bfloat16 or wider, within the bound.
A program may use at most 64 MiB of HBM per device.

v0:
```python
import jax
import jax.numpy as jnp
from jax import lax
from jax.sharding import PartitionSpec as P

KVH = 8
HD = 128
WIN = 4096


score_scale = 1.0 / 12.0
rope_base = 10000.0


def passed_along(block, axis, distance):
    devices = range(lax.axis_size(axis))
    route = [(i - distance, i) for i in devices if i - distance in devices]
    return lax.ppermute(block, axis, route)


def rms_norm(values_in, norm_gain):
    floats = values_in.astype(jnp.float32)
    square_mean = jnp.mean(floats * floats, axis=-1, keepdims=True)
    return (floats * lax.rsqrt(square_mean + 1e-06) * norm_gain).astype(jnp.bfloat16)


def rotate(heads_in, places):
    width = heads_in.shape[-1]
    half = width // 2
    inverse = jnp.exp(-jnp.log(rope_base) * jnp.arange(half, dtype=jnp.float32) * (2.0 / width))
    angle = places.astype(jnp.float32)[:, None] * inverse[None, :]
    cosine = jnp.cos(angle)[:, None, :]
    sine = jnp.sin(angle)[:, None, :]
    lower = heads_in[..., :half]
    upper = heads_in[..., half:]
    return jnp.concatenate([lower * cosine - upper * sine, upper * cosine + lower * sine], axis=-1)


def per_device(tokens, norm_gain, query_weight, key_weight, value_weight, out_weight, positions):
    tok_rows = tokens.shape[0]
    col_count = lax.axis_size("col")
    seq_count = lax.axis_size("seq")
    seq_index = lax.axis_index("seq")
    kv_local = KVH // col_count
    whole = lax.all_gather(tokens, "col", axis=1, tiled=True)
    normed = rms_norm(whole, norm_gain)
    all_places = lax.all_gather(positions, "seq", axis=0, tiled=True)
    pieces = (
        lax.all_gather(query_weight, "seq", axis=0, tiled=True),
        lax.all_gather(key_weight, "seq", axis=0, tiled=True),
        lax.all_gather(value_weight, "seq", axis=0, tiled=True),
    )
    columns = normed
    query_raw, key_raw, value_raw = tuple(
        (jnp.dot(columns, piece, preferred_element_type=jnp.float32) for piece in pieces)
    )
    queries = (
        rotate(query_raw.reshape(tok_rows, 2 * kv_local, HD), positions)
        .astype(jnp.bfloat16)
        .reshape(tok_rows, kv_local, 2, HD)
    )
    keys = (
        rotate(key_raw.reshape(tok_rows, kv_local, HD), positions)
        .astype(jnp.bfloat16)
        .reshape(tok_rows, kv_local * HD)
    )
    values = value_raw.astype(jnp.bfloat16)
    packed = jnp.stack([keys, values])
    reach = min(WIN // tok_rows, seq_count - 1)
    blocks = [packed]
    current = packed
    for step in range(reach):
        current = passed_along(current, "seq", 1)
        blocks.insert(0, current)
    window = jnp.concatenate(blocks, axis=1)
    span = (reach + 1) * tok_rows
    places_pad = jnp.concatenate([jnp.zeros((reach * tok_rows,), jnp.int32), all_places], axis=0)
    key_places = lax.dynamic_slice_in_dim(places_pad, seq_index * tok_rows, span, 0)
    key_index = (seq_index - reach) * tok_rows + jnp.arange(span, dtype=jnp.int32)
    query_index = seq_index * tok_rows + jnp.arange(tok_rows, dtype=jnp.int32)
    group = 1
    for candidate in range(1, reach + 2):
        if (reach + 1) % candidate == 0 and candidate * tok_rows <= max(512, tok_rows):
            group = candidate
    key_rows = group * tok_rows
    key_blocks = span // key_rows
    keys_blocked = window[0].reshape(key_blocks, key_rows, kv_local, HD)[::-1]
    values_blocked = window[1].reshape(key_blocks, key_rows, kv_local, HD)[::-1]
    places_blocked = key_places.reshape(key_blocks, key_rows)[::-1]
    index_blocked = key_index.reshape(key_blocks, key_rows)[::-1]

    def attend(carry, block):
        largest, total, summed = carry
        key_part, value_part, place_part, index_part = block
        scores = (
            jnp.einsum("qgeh,kgh->qgek", queries, key_part, preferred_element_type=jnp.float32)
            * score_scale
        )
        distance = query_index[:, None] - index_part[None, :]
        visible = (index_part[None, :] >= 0) & (distance >= 0) & (distance < WIN)
        visible = visible & (positions[:, None] - place_part[None, :] == distance)
        scores = jnp.where(visible[:, None, None, :], scores, -1e30)
        newest = jnp.maximum(largest, jnp.max(scores, axis=-1))
        factor = jnp.exp(largest - newest)
        weights = jnp.exp(scores - newest[..., None])
        total = total * factor + jnp.sum(weights, axis=-1)
        summed = summed * factor[..., None] + jnp.einsum(
            "qgek,kgh->qgeh",
            weights.astype(jnp.bfloat16),
            value_part,
            preferred_element_type=jnp.float32,
        )
        return ((newest, total, summed), None)

    start_state = (
        jnp.full((tok_rows, kv_local, 2), -1e30, jnp.float32),
        jnp.zeros((tok_rows, kv_local, 2), jnp.float32),
        jnp.zeros((tok_rows, kv_local, 2, HD), jnp.float32),
    )
    final_state, unused = lax.scan(
        attend, start_state, (keys_blocked, values_blocked, places_blocked, index_blocked)
    )
    attended = (
        (final_state[2] / final_state[1][..., None])
        .astype(jnp.bfloat16)
        .reshape(tok_rows, 2 * kv_local * HD)
    )
    mixed = lax.all_gather(attended, "col", axis=1, tiled=True)
    columns = mixed
    projected = jnp.dot(
        columns,
        lax.all_gather(out_weight, "seq", axis=0, tiled=True),
        preferred_element_type=jnp.float32,
    )
    return (tokens.astype(jnp.float32) + projected).astype(jnp.bfloat16)


def solution(mesh):
    return jax.shard_map(
        per_device,
        mesh=mesh,
        in_specs=(
            P(("grp", "seq"), "col"),
            P(),
            P("seq", "col"),
            P("seq", "col"),
            P("seq", "col"),
            P("seq", "col"),
            P(("grp", "seq")),
        ),
        out_specs=P(("grp", "seq"), "col"),
        check_vma=False,
    )
```

profile of v0, /device:TPU:31, one launch (start us, length us, event | category | flops | bytes accessed | tf_op | source)
XLA Modules:
  0.0 394.8 jit_solution(13647404061947721689)
XLA Ops:
  10.6 36.2 %all-gather.8.cloned.1.call-done = bf16[512,4608]{1,0:T(8,128)(2,1)} async-done(((bf16[512,1152]{1,0:T(8,128)(2,1)}), bf16[512,4608]{1,0:T(8,128)(2,1)}) %all-gather.8.cloned.1.call-update) | async-done | bytes 4718608 | tf_op jit(solution)/shard_map/all_gather | solution.py:45
  46.8 3.3 fusion.31
  50.1 47.2 %all-gather.10.cloned.1.call-done = bf16[4608,256]{1,0:T(8,128)(2,1)} async-done(((bf16[1152,256]{1,0:T(8,128)(2,1)}), bf16[4608,256]{1,0:T(8,128)(2,1)}) %all-gather.10.cloned.1.call-update) | async-done | bytes 2359312 | tf_op jit(solution)/shard_map/all_gather | solution.py:50
  97.4 4.8 %fusion.39 = f32[512,256]{0,1:T(8,128)S(1)} fusion(bf16[4608,256]{1,0:T(8,128)(2,1)} %all-gather.10.cloned.1.call-done, bf16[512,4608]{1,0:T(8,128)(2,1)} %all-gather.8.cloned.1.call-done, f32[4608]{0:T(1024)S(1)} %copy-done.5, f32[512]{0:T(512)S(1)} %add_rsqrt_fusion), kind=kOutput, calls=%fused_computation.64 | convolution fusion | flops 1217396736 | bytes 7622656 | tf_op jit(solution)/shard_map/dot_general | solution.py:55
  102.5 45.8 %all-gather.12.cloned.1.call-done = bf16[4608,256]{1,0:T(8,128)(2,1)} async-done(((bf16[1152,256]{1,0:T(8,128)(2,1)}), bf16[4608,256]{1,0:T(8,128)(2,1)}) %all-gather.12.cloned.1.call-update) | async-done | bytes 2359312 | tf_op jit(solution)/shard_map/all_gather | solution.py:51
  148.3 4.6 %fusion.35 = bf16[1,512,256]{2,1,0:T(8,128)(2,1)S(1)} fusion(bf16[4608,256]{1,0:T(8,128)(2,1)} %all-gather.12.cloned.1.call-done, bf16[512,4608]{1,0:T(8,128)(2,1)} %all-gather.8.cloned.1.call-done, f32[4608]{0:T(1024)S(1)} %copy-done.5, f32[512]{0:T(512)S(1)} %add_rsqrt_fusion), kind=kOutput, calls=%fused_computation.47 | convolution fusion | flops 1217527808 | bytes 7360512 | tf_op jit(solution)/shard_map/dot_general | solution.py:55
  154.2 27.1 %collective-permute-done = bf16[2,512,256]{2,1,0:T(8,128)(2,1)S(1)} collective-permute-done((bf16[2,512,256]{2,1,0:T(8,128)(2,1)S(1)}, bf16[2,512,256]{2,1,0:T(8,128)(2,1)S(1)}, u32[]{:S(2)}, u32[]{:S(2)}) %collective-permute-start) | collective-permute-done | bytes 524320 | tf_op jit(solution)/shard_map/ppermute | solution.py:18
  182.8 41.1 %all-gather = s32[4,1,512]{2,1,0:T(1,128)S(1)} all-gather(s32[1,1,512]{2,1,0:T(1,128)S(1)} %bitcast.75), channel_id=1, replica_groups=mesh['grp'=2,'seq'=4,'col'=4] {'seq'}, dimensions={0}, use_global_device_ids=true | all-gather | bytes 10240 | tf_op jit(solution)/shard_map/all_gather | solution.py:47
  225.9 1.5 collective-permute-start.2
  227.3 40.2 %all-gather.14.cloned.1.call-done = bf16[4608,512]{1,0:T(8,128)(2,1)} async-done(((bf16[1152,512]{1,0:T(8,128)(2,1)}), bf16[4608,512]{1,0:T(8,128)(2,1)}) %all-gather.14.cloned.1.call-update) | async-done | bytes 4718608 | tf_op jit(solution)/shard_map/all_gather | solution.py:49
  267.5 6.9 %fusion.36 = f32[512,512]{0,1:T(8,128)S(1)} fusion(bf16[4608,512]{1,0:T(8,128)(2,1)} %all-gather.14.cloned.1.call-done, bf16[512,4608]{1,0:T(8,128)(2,1)} %all-gather.8.cloned.1.call-done, f32[4608]{0:T(1024)S(1)} %copy-done.5, f32[512]{0:T(512)S(1)} %add_rsqrt_fusion), kind=kOutput, calls=%fused_computation.63 | convolution fusion | flops 2425356288 | bytes 10506240 | tf_op jit(solution)/shard_map/dot_general | solution.py:55
  275.4 1.4 maximum_maximum_fusion
  278.5 1.4 reshape_squeeze.7
  279.9 2.0 copy.19
  281.9 2.2 rev.15
  284.1 47.9 %while.15 = (s32[]{:T(128)}, f32[512,2,2]{0,2,1:T(2,128)S(1)}, f32[512,2,2]{0,2,1:T(2,128)S(1)}, f32[512,2,2,128]{0,3,2,1:T(8,128)}, s32[4,512]{1,0:T(4,128)}, /...) while((s32[]{:T(128)}, f32[512,2,2]{0,2,1:T(2,128)S(1)}, ...), condition=%wide.region_4.5_spmd.clone, body=%wide.region_1.4_spmd.clone.sunk | while | flops 551300096 | bytes 33705652 | solution.py:120
  286.2 2.9 fusion.61
  289.1 3.3 fusion.63
  292.6 3.3 fusion.65
  297.9 2.9 fusion.61
  300.7 3.3 fusion.63
  304.2 3.7 fusion.65
  309.9 2.9 fusion.61
  312.8 3.3 fusion.63
  316.2 3.7 fusion.65
  321.9 2.9 fusion.61
  324.8 3.3 fusion.63
  328.3 3.7 fusion.65
  332.0 2.1 divide_convert_fusion
  334.2 22.5 %all-gather.18.cloned.1.call-done = bf16[2048,1152]{1,0:T(8,128)(2,1)} async-done(((bf16[512,1152]{1,0:T(8,128)(2,1)}), bf16[2048,1152]{1,0:T(8,128)(2,1)}) %all-gather.18.cloned.1.call-update) | async-done | bytes 4718608 | tf_op jit(solution)/shard_map/all_gather | solution.py:132
  356.7 24.3 %all-gather.16.cloned.1.call-done = bf16[512,2048]{0,1:T(8,128)(2,1)} async-done(((bf16[512,512]{0,1:T(8,128)(2,1)}), bf16[512,2048]{0,1:T(8,128)(2,1)}) %all-gather.16.cloned.1.call-update) | async-done | bytes 2097168 | tf_op jit(solution)/shard_map/all_gather | solution.py:128
  381.0 6.9 %fusion.34 = bf16[512,1152]{1,0:T(8,128)(2,1)} fusion(bf16[512,2048]{0,1:T(8,128)(2,1)} %all-gather.16.cloned.1.call-done, bf16[2048,1152]{1,0:T(8,128)(2,1)} %all-gather.18.cloned.1.call-done, bf16[512,1152]{1,0:T(8,128)(2,1)S(1)} %copy-done.1), kind=kOutput, calls=%fused_computation.44 | convolution fusion | flops 2417688576 | bytes 9175040 | tf_op jit(solution)/shard_map/dot_general | solution.py:130
  (87 shorter events, 20.4 us)
Async XLA Ops:
  6.5 40.3 %all-gather.8.cloned.1.call-start = ((), (), s32[]{:S(2)}) async-start(), calls=%async_computation | async-start | bytes 5898240 | tf_op jit(solution)/shard_map/all_gather | solution.py:45
  6.5 90.9 %copy-start.5 = (f32[4608]{0:T(1024)S(1)}, f32[4608]{0:T(1024)}, u32[]{:S(2)}) copy-start(f32[4608]{0:T(1024)} %param.10) | copy-start | bytes 55300
  7.3 90.1 %all-gather.10.cloned.1.call-start = ((), (), s32[]{:S(2)}) async-start(), calls=%async_computation.1 | async-start | bytes 2949120 | tf_op jit(solution)/shard_map/all_gather | solution.py:50
  8.0 140.3 %all-gather.12.cloned.1.call-start = ((), (), s32[]{:S(2)}) async-start(), calls=%async_computation.2 | async-start | bytes 2949120 | tf_op jit(solution)/shard_map/all_gather | solution.py:51
  8.7 258.8 %all-gather.14.cloned.1.call-start = ((), (), s32[]{:S(2)}) async-start(), calls=%async_computation.3 | async-start | bytes 5898240 | tf_op jit(solution)/shard_map/all_gather | solution.py:49
  9.3 347.4 %all-gather.18.cloned.1.call-start = ((), (), s32[]{:S(2)}) async-start(), calls=%async_computation.5 | async-start | bytes 5898240 | tf_op jit(solution)/shard_map/all_gather | solution.py:132
  102.5 80.2 %copy-start.3 = (s32[512]{0:T(512)S(1)}, s32[512]{0:T(512)}, u32[]{:S(2)}) copy-start(s32[512]{0:T(512)} %param.15) | copy-start | bytes 6148
  152.9 28.4 %collective-permute-start = (bf16[2,512,256]{2,1,0:T(8,128)(2,1)S(1)}, bf16[2,512,256]{2,1,0:T(8,128)(2,1)S(1)}, u32[]{:S(2)}, u32[]{:S(2)}) collective-permute-start(bf16[2,512,256]{2,1,0:T(8,128)(2,1)S(1)} %pad_maximum_fusion), channel_id=1, source_target_pairs={{0,4},{4,8},{8,12},{1,5},{5,9},{9,13},{2,6},{6,10},{10,14},{3,7},{... | collective-permute-start | bytes 1572872 | tf_op jit(solution)/shard_map/ppermute | solution.py:18
  181.3 44.5 %collective-permute-start.1 = (bf16[2,512,256]{2,1,0:T(8,128)(2,1)S(1)}, bf16[2,512,256]{2,1,0:T(8,128)(2,1)S(1)}, u32[]{:S(2)}, u32[]{:S(2)}) collective-permute-start(bf16[2,512,256]{2,1,0:T(8,128)(2,1)S(1)} %collective-permute-done), channel_id=1, source_target_pairs={{0,4},{4,8},{8,12},{1,5},{5,9},{9,13},{2,6},{6,10},{10,14},{3,7},{... | collective-permute-start | bytes 1572872 | tf_op jit(solution)/shard_map/ppermute | solution.py:18
  182.7 198.4 %all-gather.16.cloned.1.call-start = ((), (), s32[]{:S(2)}) async-start(), calls=%async_computation.4 | async-start | bytes 2621440 | tf_op jit(solution)/shard_map/all_gather | solution.py:128
  225.9 49.6 %collective-permute-start.2 = (bf16[2,512,256]{2,1,0:T(8,128)(2,1)S(1)}, bf16[2,512,256]{2,1,0:T(8,128)(2,1)}, u32[]{:S(2)}, u32[]{:S(2)}) collective-permute-start(bf16[2,512,256]{2,1,0:T(8,128)(2,1)S(1)} %collective-permute-done.1), channel_id=1, source_target_pairs={{0,4},{4,8},{8,12},{1,5},{5,9},{9,13},{2,6},{6,10},{10,14},{3,7},{... | collective-permute-start | bytes 1572872 | tf_op jit(solution)/shard_map/ppermute | solution.py:18
  278.4 5.8 %copy-start.2 = (f32[512,2,2]{0,2,1:T(2,128)S(1)}, f32[512,2,2]{0,2,1:T(2,128)}, u32[]{:S(2)}) copy-start(f32[512,2,2]{0,2,1:T(2,128)} %custom-call.1) | copy-start | bytes 24580
  278.4 5.8 %copy-start.4 = (s32[512]{0:T(512)S(1)}, s32[512]{0:T(512)}, u32[]{:S(2)}) copy-start(s32[512]{0:T(512)} %param.15) | copy-start | bytes 6148
  284.1 96.9 %copy-start.1 = (bf16[512,1152]{1,0:T(8,128)(2,1)S(1)}, bf16[512,1152]{1,0:T(8,128)(2,1)}, u32[]{:S(2)}) copy-start(bf16[512,1152]{1,0:T(8,128)(2,1)} %param.9) | copy-start | bytes 3538948
  289.1 3.5 copy-start
  300.7 3.5 copy-start
  312.7 3.5 copy-start
  324.8 3.5 copy-start
Sparse Core Ops, SparseCore 0:
  8.9 37.8 all-gather.7
  48.4 48.9 all-gather.9
  99.0 49.2 all-gather.11
  149.7 117.7 all-gather.13
  268.9 87.7 all-gather.17
  358.1 22.8 all-gather.15
where the time goes:
time: 398 us; the launch traced here: 395 us
  waiting for transfers between devices  246 us (62%)
  matrix products  49.1 us (12%)
  blocking collectives  41.1 us (10%)
  other arithmetic  27.6 us (7%)
  between operations  13.7 us (3%)
  local copies, waits for them, and re-layouts  12.9 us (3%)
  starting transfers between devices  4.23 us (1%)
    all_gather x1, waiting for transfers between devices, per_device(): lax.all_gather(key_weight, 'seq', axis=0, tiled=True)  47.2 us
    all_gather x1, waiting for transfers between devices, per_device(): lax.all_gather(value_weight, 'seq', axis=0, tiled=True)  45.8 us
    all_gather x1, blocking collectives, per_device(): all_places = lax.all_gather(positions, 'seq', axis=0, tiled=True)  41.1 us
    all_gather x1, waiting for transfers between devices, per_device(): lax.all_gather(query_weight, 'seq', axis=0, tiled=True)  40.2 us
    all_gather x1, waiting for transfers between devices, per_device(): whole = lax.all_gather(tokens, 'col', axis=1, tiled=True)  36.2 us
    ppermute x3, waiting for transfers between devices, passed_along(): return lax.ppermute(block, axis, route)  27.1 us
    all_gather x1, waiting for transfers between devices, per_device(): mixed = lax.all_gather(attended, 'col', axis=1, tiled=True)  24.3 us
    all_gather x1, waiting for transfers between devices, per_device(): lax.all_gather(out_weight, 'seq', axis=0, tiled=True)  22.5 us
  transfers between devices with their start and end apart: 9, of which 7 were waited for; matrix products, arithmetic and copies ran while one was open for 21% of the time, Pallas kernels for 0%

commit v1 on v0

--- a/solution.py
+++ b/solution.py
@@ -1,6 +1,8 @@
 import jax
 import jax.numpy as jnp
 from jax import lax
+from jax.experimental import pallas as pl
+from jax.experimental.pallas import tpu as pltpu
 from jax.sharding import PartitionSpec as P
 
 KVH = 8
@@ -135,9 +137,346 @@
     return (tokens.astype(jnp.float32) + projected).astype(jnp.bfloat16)
 
 
+MESH = pl.DeviceIdType.MESH
+N_SEQ = 4
+N_COL = 4
+LOG2E = 1.4426950408889634
+KEY, VAL, QUE, OUT = range(4)
+
+
+def block_kernel(
+    tok, gain, kw, vw, qw, ow, cosine, sine, first,
+    out,
+    x_all, normed, wk, wv, wq, wo, keys, values, queries, mixed,
+    z_send, z_recv, y_send, y_recv, t_send, t_recv, l_sem, k_send, k_recv, a_send, a_recv,
+):
+    g = lax.axis_index("grp")
+    s = lax.axis_index("seq")
+    c = lax.axis_index("col")
+    sources = (kw, vw, qw, ow)
+    gathered = (wk, wv, wq, wo)
+    signs = (1, -1)
+    rows = tok.shape[0]
+    feats = tok.shape[1]
+    kv_cols = kw.shape[1]
+    kv_local = kv_cols // HD
+
+    def half(a, which):
+        size = sources[a].shape[0] // 2
+        return pl.ds(pl.multiple_of(which * size, 16), size)
+
+    def came(d, r):
+        return (s - r >= 0) if d == 0 else (s + r < N_SEQ)
+
+    def has_next(d):
+        return (s + 1 < N_SEQ) if d == 0 else (s >= 1)
+
+    def z_copy(a, d, r):
+        b = s - signs[d] * (r - 1)
+        mine = half(a, g)
+        src = sources[a].at[mine] if r == 1 else gathered[a].at[b, mine]
+        return pltpu.make_async_remote_copy(
+            src, gathered[a].at[b, mine], z_send.at[a, d, r - 1], z_recv.at[a, d, r - 1],
+            device_id={"seq": s + signs[d]}, device_id_type=MESH)
+
+    def z_wait(a, d, r):
+        ref = gathered[a].at[s - signs[d] * r, half(a, g)]
+        pltpu.make_async_remote_copy(
+            ref, ref, z_send.at[a, d, r - 1], z_recv.at[a, d, r - 1],
+            device_id={"seq": s - signs[d]}, device_id_type=MESH).wait_recv()
+
+    def y_copy(a, d, r, which):
+        ref = gathered[a].at[s - signs[d] * r, half(a, which)]
+        return pltpu.make_async_remote_copy(
+            ref, ref, y_send.at[a, d, r - 1], y_recv.at[a, d, r - 1],
+            device_id={"grp": 1 - g}, device_id_type=MESH)
+
+    def begin(names):
+        for d in range(2):
+            @pl.when(has_next(d))
+            def _():
+                for a in names:
+                    z_copy(a, d, 1).start()
+
+    def pass_on(names, r):
+        for d in range(2):
+            @pl.when(came(d, r))
+            def _():
+                for a in names:
+                    z_wait(a, d, r)
+                    if r < N_SEQ - 1:
+                        @pl.when(has_next(d))
+                        def _():
+                            z_copy(a, d, r + 1).start()
+                    y_copy(a, d, r, g).start()
+
+    def arrived(names):
+        for a in names:
+            for d in range(2):
+                for r in range(1, N_SEQ):
+                    @pl.when(came(d, r))
+                    def _():
+                        y_copy(a, d, r, 1 - g).wait_recv()
+
+    def col_copy(src, dst_of, sender, k, send, recv):
+        return pltpu.make_async_remote_copy(
+            src, dst_of(sender), send, recv,
+            device_id={"col": lax.rem(c + k, N_COL)}, device_id_type=MESH)
+
+    def token_copy(k, sender):
+        return col_copy(tok, lambda i: x_all.at[i], sender, k, t_send.at[k - 1], t_recv.at[k - 1])
+
+    def mixed_copy(k, e, sender):
+        part = lambda i: mixed.at[i, :, pl.ds(e * 2 * HD, 2 * HD)]
+        return col_copy(part(c), part, sender, k, a_send.at[k - 1, e], a_recv.at[k - 1, e])
+
+    def kv_copy(which, d):
+        ref = (keys, values)[which]
+        return pltpu.make_async_remote_copy(
+            ref.at[0], ref.at[d], k_send.at[which, d - 1], k_recv.at[which, d - 1],
+            device_id={"seq": s + d}, device_id_type=MESH)
+
+    barrier = pltpu.get_barrier_semaphore()
+    pl.semaphore_signal(barrier, inc=1, device_id={"grp": 1 - g}, device_id_type=MESH)
+    for k in range(1, N_COL):
+        pl.semaphore_signal(
+            barrier, inc=1, device_id={"col": lax.rem(c + k, N_COL)}, device_id_type=MESH)
+    for d in (-2, -1, 1, 2):
+        @pl.when((s + d >= 0) & (s + d < N_SEQ))
+        def _():
+            pl.semaphore_signal(barrier, inc=1, device_id={"seq": s + d}, device_id_type=MESH)
+    inner = jnp.where((s >= 1) & (s < N_SEQ - 1), 1, 0)
+    pl.semaphore_wait(barrier, N_COL + 2 + inner)
+
+    begin((KEY, VAL))
+    for k in range(1, N_COL):
+        token_copy(k, c).start()
+    local = [pltpu.make_async_copy(tok, x_all.at[c], l_sem.at[4])]
+    for a in (KEY, VAL, QUE, OUT):
+        local.append(pltpu.make_async_copy(sources[a], gathered[a].at[s], l_sem.at[a]))
+    for copy in local:
+        copy.start()
+
+    for d in (1, 2):
+        @pl.when(s < d)
+        def _():
+            keys[d] = jnp.zeros_like(keys[d])
+            values[d] = jnp.zeros_like(values[d])
+
+    pass_on((KEY, VAL), 1)
+    begin((QUE,))
+    pass_on((KEY, VAL), 2)
+    pass_on((QUE,), 1)
+    begin((OUT,))
+    pass_on((KEY, VAL), 3)
+
+    for copy in local:
+        copy.wait()
+    for k in range(1, N_COL):
+        token_copy(k, lax.rem(c + N_COL - k, N_COL)).wait_recv()
+
+    step = 64
+
+    def norm_rows(t, carry):
+        at = pl.ds(pl.multiple_of(t * step, step), step)
+        total = jnp.zeros((step, 1), jnp.float32)
+        for b in range(N_COL):
+            f = x_all[b, at, :].astype(jnp.float32)
+            total = total + jnp.sum(f * f, axis=-1, keepdims=True)
+        scale = lax.rsqrt(total / (N_COL * feats) + 1e-06)
+        for b in range(N_COL):
+            f = x_all[b, at, :].astype(jnp.float32)
+            normed[b, at, :] = (f * scale * gain[b]).astype(jnp.bfloat16)
+        return carry
+
+    lax.fori_loop(0, rows // step, norm_rows, 0)
+    pass_on((QUE,), 2)
+    arrived((KEY, VAL))
+
+    tile = 256
+
+    def project(at, weight, lo):
+        total = jnp.dot(normed[0, at, :], weight[0, :, lo:lo + 256],
+                        preferred_element_type=jnp.float32)
+        for b in range(1, N_SEQ):
+            total = total + jnp.dot(normed[b, at, :], weight[b, :, lo:lo + 256],
+                                    preferred_element_type=jnp.float32)
+        return total
+
+    def turned(raw, at):
+        parts = []
+        for h in range(raw.shape[1] // HD):
+            u = raw[:, h * HD:(h + 1) * HD]
+            swapped = jnp.concatenate([u[:, HD // 2:], u[:, :HD // 2]], axis=1)
+            parts.append(u * cosine[at, :] + swapped * sine[at, :])
+        return jnp.concatenate(parts, axis=1).astype(jnp.bfloat16)
+
+    def kv_rows(t, carry):
+        at = pl.ds(pl.multiple_of(t * tile, tile), tile)
+        keys[0, at, :] = turned(project(at, wk, 0), at)
+        values[0, at, :] = project(at, wv, 0).astype(jnp.bfloat16)
+        return carry
+
+    lax.fori_loop(0, rows // tile, kv_rows, 0)
+    for d in (1, 2):
+        @pl.when(s + d < N_SEQ)
+        def _():
+            for which in range(2):
+                kv_copy(which, d).start()
+
+    pass_on((OUT,), 1)
+    pass_on((QUE,), 3)
+    arrived((QUE,))
+
+    def q_rows(t, carry):
+        at = pl.ds(pl.multiple_of(t * tile, tile), tile)
+        for lo in range(0, qw.shape[1], 256):
+            queries[at, lo:lo + 256] = turned(project(at, wq, lo), at)
+        return carry
+
+    lax.fori_loop(0, rows // tile, q_rows, 0)
+    pass_on((OUT,), 2)
+    for d in (1, 2):
+        @pl.when(s >= d)
+        def _():
+            for which in range(2):
+                ref = (keys, values)[which].at[d]
+                pltpu.make_async_remote_copy(
+                    ref, ref, k_send.at[which, d - 1], k_recv.at[which, d - 1],
+                    device_id={"seq": s - d}, device_id_type=MESH).wait_recv()
+
+    q_tile = 128
+
+    def attend_rows(e):
+        def body(t, carry):
+            at = pl.ds(pl.multiple_of(t * q_tile, q_tile), q_tile)
+            here = s * rows + t * q_tile + lax.broadcasted_iota(jnp.int32, (q_tile, rows), 0)
+            earliest = jnp.maximum(first[at, :], 0)
+            shown = []
+            for d in range(3):
+                there = (s - d) * rows + lax.broadcasted_iota(jnp.int32, (q_tile, rows), 1)
+                ok = there >= earliest
+                if d == 0:
+                    ok = ok & (there <= here)
+                shown.append(ok)
+            lanes = slice(e * HD, (e + 1) * HD)
+            for h in range(2):
+                q_lanes = slice((2 * e + h) * HD, (2 * e + h + 1) * HD)
+                q = queries[at, q_lanes]
+                scores = []
+                for d in range(3):
+                    raw = lax.dot_general(
+                        q, keys[d, :, lanes], (((1,), (1,)), ((), ())),
+                        preferred_element_type=jnp.float32) * (score_scale * LOG2E)
+                    scores.append(jnp.where(shown[d], raw, -1e30))
+                top = jnp.maximum(jnp.maximum(scores[0], scores[1]), scores[2])
+                largest = jnp.max(top, axis=-1, keepdims=True)
+                total = jnp.zeros((q_tile, rows), jnp.float32)
+                summed = jnp.zeros((q_tile, HD), jnp.float32)
+                for d in range(3):
+                    w = jnp.exp2(scores[d] - largest)
+                    total = total + w
+                    summed = summed + jnp.dot(
+                        w.astype(jnp.bfloat16), values[d, :, lanes],
+                        preferred_element_type=jnp.float32)
+                total = jnp.sum(total, axis=-1, keepdims=True)
+                mixed[c, at, q_lanes] = (summed / total).astype(jnp.bfloat16)
+            return carry
+
+        lax.fori_loop(0, rows // q_tile, body, 0)
+
+    for e in range(kv_local):
+        attend_rows(e)
+        for k in range(1, N_COL):
+            mixed_copy(k, e, c).start()
+        if e == 0:
+            pass_on((OUT,), 3)
+
+    arrived((OUT,))
+    for k in range(1, N_COL):
+        for e in range(kv_local):
+            mixed_copy(k, e, lax.rem(c + N_COL - k, N_COL)).wait_recv()
+
+    def out_rows(t, carry):
+        at = pl.ds(pl.multiple_of(t * tile, tile), tile)
+        for lo in range(0, feats, 384):
+            cols = slice(lo, lo + 384)
+            total = jnp.dot(mixed[0, at, :], wo[0, :, cols], preferred_element_type=jnp.float32)
+            for b in range(1, N_COL):
+                total = total + jnp.dot(
+                    mixed[b, at, :], wo[b, :, cols], preferred_element_type=jnp.float32)
+            out[at, cols] = (x_all[c, at, cols].astype(jnp.float32) + total).astype(jnp.bfloat16)
+        return carry
+
+    lax.fori_loop(0, rows // tile, out_rows, 0)
+
+    for a in range(4):
+        for d in range(2):
+            for r in range(1, N_SEQ):
+                @pl.when(came(d, r - 1) & has_next(d))
+                def _():
+                    z_copy(a, d, r).wait_send()
+
+                @pl.when(came(d, r))
+                def _():
+                    y_copy(a, d, r, g).wait_send()
+    for k in range(1, N_COL):
+        token_copy(k, c).wait_send()
+        for e in range(kv_local):
+            mixed_copy(k, e, c).wait_send()
+    for d in (1, 2):
+        @pl.when(s + d < N_SEQ)
+        def _():
+            for which in range(2):
+                kv_copy(which, d).wait_send()
+
+
+def fused_device(tokens, norm_gain, query_weight, key_weight, value_weight, out_weight, positions):
+    rows, feats = tokens.shape
+    half = HD // 2
+    inverse = jnp.exp(-jnp.log(rope_base) * jnp.arange(half, dtype=jnp.float32) * (2.0 / HD))
+    angle = positions.astype(jnp.float32)[:, None] * inverse[None, :]
+    cosine = jnp.cos(angle)
+    sine = jnp.sin(angle)
+    cosine = jnp.concatenate([cosine, cosine], axis=1)
+    sine = jnp.concatenate([-sine, sine], axis=1)
+    index = lax.axis_index("seq") * rows + jnp.arange(rows, dtype=jnp.int32)
+    first = (index - positions)[:, None]
+    gain = norm_gain.reshape(N_COL, 1, feats)
+    bf16 = jnp.bfloat16
+    dma = pltpu.SemaphoreType.DMA
+    anywhere = pl.BlockSpec(memory_space=pl.ANY)
+    vmem = pl.BlockSpec(memory_space=pltpu.VMEM)
+    kv_cols = key_weight.shape[1]
+    q_cols = query_weight.shape[1]
+    return pl.pallas_call(
+        block_kernel,
+        out_shape=jax.ShapeDtypeStruct((rows, feats), bf16),
+        in_specs=[anywhere, vmem, anywhere, anywhere, anywhere, anywhere, vmem, vmem, vmem],
+        out_specs=vmem,
+        scratch_shapes=[
+            pltpu.VMEM((N_COL, rows, feats), bf16),
+            pltpu.VMEM((N_COL, rows, feats), bf16),
+            pltpu.VMEM((N_SEQ,) + key_weight.shape, bf16),
+            pltpu.VMEM((N_SEQ,) + value_weight.shape, bf16),
+            pltpu.VMEM((N_SEQ,) + query_weight.shape, bf16),
+            pltpu.VMEM((N_SEQ,) + out_weight.shape, bf16),
+            pltpu.VMEM((3, rows, kv_cols), bf16),
+            pltpu.VMEM((3, rows, kv_cols), bf16),
+            pltpu.VMEM((rows, q_cols), bf16),
+            pltpu.VMEM((N_COL, rows, q_cols), bf16),
+            dma((4, 2, 3)), dma((4, 2, 3)), dma((4, 2, 3)), dma((4, 2, 3)),
+            dma((3,)), dma((3,)), dma((5,)), dma((2, 2)), dma((2, 2)), dma((3, 2)), dma((3, 2)),
+        ],
+        compiler_params=pltpu.CompilerParams(
+            collective_id=0, has_side_effects=True, vmem_limit_bytes=52 * 1024 * 1024),
+    )(tokens, gain, key_weight, value_weight, query_weight, out_weight, cosine, sine, first)
+
+
 def solution(mesh):
+    small = (mesh.shape["grp"], mesh.shape["seq"], mesh.shape["col"]) == (2, N_SEQ, N_COL)
     return jax.shard_map(
-        per_device,
+        fused_device if small else per_device,
         mesh=mesh,
         in_specs=(
             P(("grp", "seq"), "col"),

time: 398 us -> 167 us (0.42)
  waiting for transfers between devices: 246 us -> 0 us
  Pallas kernels: 0 us -> 161 us
  matrix products: 49.1 us -> 0 us
  blocking collectives: 41.1 us -> 0 us
  other arithmetic: 27.6 us -> 1.97 us
  between operations: 13.7 us -> 0.06 us
  local copies, waits for them, and re-layouts: 12.9 us -> 3.28 us
  starting transfers between devices: 4.23 us -> 0 us
    all_gather x6 -> x0, waiting for transfers between devices: 216 us -> none  [the longest x1 47.2 us: per_device(): lax.all_gather(key_weight, 'seq', axis=0, tiled=True)]
    pallas_call x0 -> x1, Pallas kernels: none -> 161 us  [fused_device(): pl.pallas_call(block_kernel, out_shape=jax.ShapeDtypeStruct((rows, feats)...]
    dot_general x12 -> x0, matrix products: 49.1 us -> none  [the longest x3 16.3 us: per_device(): jnp.dot(columns, piece, preferred_element_type=jnp.float32)]
    all_gather x1 -> x0, blocking collectives: 41.1 us -> none  [per_device(): all_places = lax.all_gather(positions, 'seq', axis=0, tiled=True)]
    ppermute x3 -> x0, waiting for transfers between devices: 27.1 us -> none  [passed_along(): return lax.ppermute(block, axis, route)]
    reduce_sum x5 -> x0, other arithmetic: 16.4 us -> none  [the longest x4 13.1 us: attend(): total = total * factor + jnp.sum(weights, axis=-1)]
    another operation x7 -> x0, local copies, waits for them, and re-layouts: 4.46 us -> none  [the longest x2 3.4 us: per_device(): values_blocked = window[1].reshape(key_blocks, key_rows, kv_local, HD)[::-1]]
    ppermute x3 -> x0, starting transfers between devices: 4.03 us -> none  [passed_along(): return lax.ppermute(block, axis, route)]
  transfers between devices with their start and end apart: 9 -> 0, of which waited for: 7 -> 0; matrix products, arithmetic and copies ran while one was open for 21% -> 0% of each run, Pallas kernels for 0% -> 0%
where the time goes in v1:
time: 167 us
  Pallas kernels  161 us (96%)
  local copies, waits for them, and re-layouts  3.28 us (2%)
  other arithmetic  1.97 us (1%)
    pallas_call x1, Pallas kernels, fused_device(): pl.pallas_call(block_kernel, out_shape=jax.ShapeDtypeStruct((rows, feats)...  161 us

profile of v1, /device:TPU:31, one launch (start us, length us, event | category | flops | bytes accessed | tf_op | source)
XLA Modules:
  0.0 166.7 jit_solution(17146926684646279648)
XLA Ops:
  0.0 0.8 add_subtract_fusion
  0.8 0.7 reshape.9.gain
  1.5 0.0 copy-start
  1.5 0.0 copy-start.1
  1.5 0.1 copy.8.first
  1.7 1.0 fusion
  2.7 0.2 pad_maximum_fusion
  2.9 0.0 copy-done
  2.9 0.0 copy-done.1
  2.9 161.4 %shard_map.73 = bf16[512,1152]{1,0:T(8,128)(2,1)} custom-call(bf16[512,1152]{1,0:T(8,128)(2,1)} %tok.1, f32[4,1,1152]{2,1,0:T(1,128)S(1)} %reshape.9.gain, bf16[1152,256]{1,0:T(8,128)(2,1)S(1)} %copy-done, bf16[1152,256]{1,0:T(8,128)(2,1)S(1)} %copy-done.1, bf16[1152,512]{1,0:T(8,128)(2,1)} %qw.1, bf16[512,1152]{1,0:T(8,128)(2,1)} %ow.1, ...), custom_call_target="tpu_custom_call" | custom-call | tf_op jit(solution)/shard_map/pallas_call | solution.py:452
  164.3 2.4 %copy.10 = bf16[512,1152]{1,0:T(8,128)(2,1)} copy(bf16[512,1152]{1,0:T(8,128)(2,1)} %shard_map.73) | data formatting | bytes 2359296
  (1 shorter events, 0.0 us)
Async XLA Ops:
  1.5 1.4 copy-start
  1.5 1.4 copy-start.1

commit v2 on v1

--- a/solution.py
+++ b/solution.py
@@ -142,6 +142,8 @@
 N_COL = 4
 LOG2E = 1.4426950408889634
 KEY, VAL, QUE, OUT = range(4)
+PIECES = ((KEY, 0, 1), (VAL, 0, 1), (QUE, 0, 2), (QUE, 1, 2), (OUT, 0, 2), (OUT, 1, 2))
+K_0, V_0, Q_0, Q_1, O_0, O_1 = range(6)
 
 
 def block_kernel(
@@ -161,9 +163,13 @@
     kv_cols = kw.shape[1]
     kv_local = kv_cols // HD
 
-    def half(a, which):
-        size = sources[a].shape[0] // 2
-        return pl.ds(pl.multiple_of(which * size, 16), size)
+    def half(p, which):
+        a, part, parts = PIECES[p]
+        size = sources[a].shape[0] // (2 * parts)
+        return pl.ds(pl.multiple_of((which * parts + part) * size, 16), size)
+
+    def place(p, b, which):
+        return gathered[PIECES[p][0]].at[b, half(p, which)]
 
     def came(d, r):
         return (s - r >= 0) if d == 0 else (s + r < N_SEQ)
@@ -171,24 +177,24 @@
     def has_next(d):
         return (s + 1 < N_SEQ) if d == 0 else (s >= 1)
 
-    def z_copy(a, d, r):
+    def z_copy(p, d, r):
         b = s - signs[d] * (r - 1)
-        mine = half(a, g)
-        src = sources[a].at[mine] if r == 1 else gathered[a].at[b, mine]
+        ref = place(p, b, g)
+        src = sources[PIECES[p][0]].at[half(p, g)] if r == 1 else ref
         return pltpu.make_async_remote_copy(
-            src, gathered[a].at[b, mine], z_send.at[a, d, r - 1], z_recv.at[a, d, r - 1],
+            src, ref, z_send.at[p, d, r - 1], z_recv.at[p, d, r - 1],
             device_id={"seq": s + signs[d]}, device_id_type=MESH)
 
-    def z_wait(a, d, r):
-        ref = gathered[a].at[s - signs[d] * r, half(a, g)]
+    def z_wait(p, d, r):
+        ref = place(p, s - signs[d] * r, g)
         pltpu.make_async_remote_copy(
-            ref, ref, z_send.at[a, d, r - 1], z_recv.at[a, d, r - 1],
+            ref, ref, z_send.at[p, d, r - 1], z_recv.at[p, d, r - 1],
             device_id={"seq": s - signs[d]}, device_id_type=MESH).wait_recv()
 
-    def y_copy(a, d, r, which):
-        ref = gathered[a].at[s - signs[d] * r, half(a, which)]
+    def y_copy(p, d, r, which):
+        ref = place(p, s - signs[d] * r, which)
         return pltpu.make_async_remote_copy(
-            ref, ref, y_send.at[a, d, r - 1], y_recv.at[a, d, r - 1],
+            ref, ref, y_send.at[p, d, r - 1], y_recv.at[p, d, r - 1],
             device_id={"grp": 1 - g}, device_id_type=MESH)
 
     def begin(names):
@@ -218,17 +224,25 @@
                     def _():
                         y_copy(a, d, r, 1 - g).wait_recv()
 
-    def col_copy(src, dst_of, sender, k, send, recv):
+    core = c + 1 - 2 * lax.rem(c, 2)
+    across = lax.rem(c + 2, N_COL)
+    far = lax.rem(core + 2, N_COL)
+
+    def token_copy(k, block):
+        src = x_all.at[block] if k == 2 else tok
         return pltpu.make_async_remote_copy(
-            src, dst_of(sender), send, recv,
-            device_id={"col": lax.rem(c + k, N_COL)}, device_id_type=MESH)
-
-    def token_copy(k, sender):
-        return col_copy(tok, lambda i: x_all.at[i], sender, k, t_send.at[k - 1], t_recv.at[k - 1])
-
-    def mixed_copy(k, e, sender):
-        part = lambda i: mixed.at[i, :, pl.ds(e * 2 * HD, 2 * HD)]
-        return col_copy(part(c), part, sender, k, a_send.at[k - 1, e], a_recv.at[k - 1, e])
+            src, x_all.at[block], t_send.at[k], t_recv.at[k],
+            device_id={"col": across if k == 0 else core}, device_id_type=MESH)
+
+    def mixed_copy(k, e, block):
+        ref = mixed.at[block, :, pl.ds(e * 2 * HD, 2 * HD)]
+        return pltpu.make_async_remote_copy(
+            ref, ref, a_send.at[k, e], a_recv.at[k, e],
+            device_id={"col": across if k == 0 else core}, device_id_type=MESH)
+
+    def mixed_on(e):
+        mixed_copy(0, e, across).wait_recv()
+        mixed_copy(2, e, across).start()
 
     def kv_copy(which, d):
         ref = (keys, values)[which]
@@ -248,8 +262,8 @@
     inner = jnp.where((s >= 1) & (s < N_SEQ - 1), 1, 0)
     pl.semaphore_wait(barrier, N_COL + 2 + inner)
 
-    begin((KEY, VAL))
-    for k in range(1, N_COL):
+    begin((K_0, V_0))
+    for k in range(2):
         token_copy(k, c).start()
     local = [pltpu.make_async_copy(tok, x_all.at[c], l_sem.at[4])]
     for a in (KEY, VAL, QUE, OUT):
@@ -263,17 +277,20 @@
             keys[d] = jnp.zeros_like(keys[d])
             values[d] = jnp.zeros_like(values[d])
 
-    pass_on((KEY, VAL), 1)
-    begin((QUE,))
-    pass_on((KEY, VAL), 2)
-    pass_on((QUE,), 1)
-    begin((OUT,))
-    pass_on((KEY, VAL), 3)
+    pass_on((K_0, V_0), 1)
+    begin((Q_0,))
+    pass_on((K_0, V_0), 2)
+    token_copy(0, across).wait_recv()
+    token_copy(2, across).start()
+    begin((Q_1,))
+    pass_on((Q_0,), 1)
+    pass_on((K_0, V_0), 3)
+    pass_on((Q_1,), 1)
 
     for copy in local:
         copy.wait()
-    for k in range(1, N_COL):
-        token_copy(k, lax.rem(c + N_COL - k, N_COL)).wait_recv()
+    token_copy(1, core).wait_recv()
+    token_copy(2, far).wait_recv()
 
     step = 64
 
@@ -290,8 +307,8 @@
         return carry
 
     lax.fori_loop(0, rows // step, norm_rows, 0)
-    pass_on((QUE,), 2)
-    arrived((KEY, VAL))
+    pass_on((Q_0,), 2)
+    arrived((K_0, V_0))
 
     tile = 256
 
@@ -324,9 +341,13 @@
             for which in range(2):
                 kv_copy(which, d).start()
 
-    pass_on((OUT,), 1)
-    pass_on((QUE,), 3)
-    arrived((QUE,))
+    pass_on((Q_1,), 2)
+    begin((O_0,))
+    pass_on((Q_0,), 3)
+    begin((O_1,))
+    pass_on((Q_1,), 3)
+    pass_on((O_0,), 1)
+    arrived((Q_0, Q_1))
 
     def q_rows(t, carry):
         at = pl.ds(pl.multiple_of(t * tile, tile), tile)
@@ -335,7 +356,7 @@
         return carry
 
     lax.fori_loop(0, rows // tile, q_rows, 0)
-    pass_on((OUT,), 2)
+    pass_on((O_1,), 1)
     for d in (1, 2):
         @pl.when(s >= d)
         def _():
@@ -347,7 +368,7 @@
 
     q_tile = 128
 
-    def attend_rows(e):
+    def attend_rows(e, lo, hi):
         def body(t, carry):
             at = pl.ds(pl.multiple_of(t * q_tile, q_tile), q_tile)
             here = s * rows + t * q_tile + lax.broadcasted_iota(jnp.int32, (q_tile, rows), 0)
@@ -383,19 +404,30 @@
                 mixed[c, at, q_lanes] = (summed / total).astype(jnp.bfloat16)
             return carry
 
-        lax.fori_loop(0, rows // q_tile, body, 0)
+        lax.fori_loop(lo, hi, body, 0)
+
+    tiles = rows // q_tile
+
+    def share(e):
+        for k in range(2):
+            mixed_copy(k, e, c).start()
+
+    attend_rows(0, 0, tiles)
+    share(0)
+    pass_on((O_0,), 2)
+    attend_rows(1, 0, tiles // 2)
+    pass_on((O_1,), 2)
+    attend_rows(1, tiles // 2, tiles)
+    share(1)
+    mixed_on(0)
+    mixed_on(1)
+    pass_on((O_0,), 3)
+    pass_on((O_1,), 3)
 
     for e in range(kv_local):
-        attend_rows(e)
-        for k in range(1, N_COL):
-            mixed_copy(k, e, c).start()
-        if e == 0:
-            pass_on((OUT,), 3)
-
-    arrived((OUT,))
-    for k in range(1, N_COL):
-        for e in range(kv_local):
-            mixed_copy(k, e, lax.rem(c + N_COL - k, N_COL)).wait_recv()
+        mixed_copy(1, e, core).wait_recv()
+        mixed_copy(2, e, far).wait_recv()
+    arrived((O_0, O_1))
 
     def out_rows(t, carry):
         at = pl.ds(pl.multiple_of(t * tile, tile), tile)
@@ -410,7 +442,7 @@
 
     lax.fori_loop(0, rows // tile, out_rows, 0)
 
-    for a in range(4):
+    for a in range(len(PIECES)):
         for d in range(2):
             for r in range(1, N_SEQ):
                 @pl.when(came(d, r - 1) & has_next(d))
@@ -420,10 +452,10 @@
                 @pl.when(came(d, r))
                 def _():
                     y_copy(a, d, r, g).wait_send()
-    for k in range(1, N_COL):
-        token_copy(k, c).wait_send()
+    for k in range(N_COL - 1):
+        token_copy(k, across if k == 2 else c).wait_send()
         for e in range(kv_local):
-            mixed_copy(k, e, c).wait_send()
+            mixed_copy(k, e, across if k == 2 else c).wait_send()
     for d in (1, 2):
         @pl.when(s + d < N_SEQ)
         def _():
@@ -465,7 +497,7 @@
             pltpu.VMEM((3, rows, kv_cols), bf16),
             pltpu.VMEM((rows, q_cols), bf16),
             pltpu.VMEM((N_COL, rows, q_cols), bf16),
-            dma((4, 2, 3)), dma((4, 2, 3)), dma((4, 2, 3)), dma((4, 2, 3)),
+            dma((6, 2, 3)), dma((6, 2, 3)), dma((6, 2, 3)), dma((6, 2, 3)),
             dma((3,)), dma((3,)), dma((5,)), dma((2, 2)), dma((2, 2)), dma((3, 2)), dma((3, 2)),
         ],
         compiler_params=pltpu.CompilerParams(

time: 167 us -> 160 us (0.958); the launches traced: 167 us -> 157 us
  Pallas kernels: 161 us -> 152 us
    pallas_call x1, Pallas kernels: 161 us -> 152 us  [fused_device(): pl.pallas_call(block_kernel, out_shape=jax.ShapeDtypeStruct((rows, feats)...]
where the time goes in v2:
time: 160 us; the launch traced here: 157 us
  Pallas kernels  152 us (95%)
  local copies, waits for them, and re-layouts  3.28 us (2%)
  other arithmetic  1.97 us (1%)
    pallas_call x1, Pallas kernels, fused_device(): pl.pallas_call(block_kernel, out_shape=jax.ShapeDtypeStruct((rows, feats)...  152 us

profile of v2, /device:TPU:31, one launch (start us, length us, event | category | flops | bytes accessed | tf_op | source)
XLA Modules:
  0.0 157.3 jit_solution(16037724401791330165)
XLA Ops:
  0.0 0.8 add_subtract_fusion
  0.8 0.7 reshape.9.gain
  1.5 0.0 copy-start
  1.5 0.0 copy-start.1
  1.5 0.1 copy.8.first
  1.7 1.0 fusion
  2.7 0.2 pad_maximum_fusion
  2.9 0.0 copy-done
  2.9 0.0 copy-done.1
  2.9 152.0 %shard_map.73 = bf16[512,1152]{1,0:T(8,128)(2,1)} custom-call(bf16[512,1152]{1,0:T(8,128)(2,1)} %tok.1, f32[4,1,1152]{2,1,0:T(1,128)S(1)} %reshape.9.gain, bf16[1152,256]{1,0:T(8,128)(2,1)S(1)} %copy-done, bf16[1152,256]{1,0:T(8,128)(2,1)S(1)} %copy-done.1, bf16[1152,512]{1,0:T(8,128)(2,1)} %qw.1, bf16[512,1152]{1,0:T(8,128)(2,1)} %ow.1, ...), custom_call_target="tpu_custom_call" | custom-call | tf_op jit(solution)/shard_map/pallas_call | solution.py:484
  154.9 2.4 %copy.10 = bf16[512,1152]{1,0:T(8,128)(2,1)} copy(bf16[512,1152]{1,0:T(8,128)(2,1)} %shard_map.73) | data formatting | bytes 2359296
  (1 shorter events, 0.0 us)
Async XLA Ops:
  1.5 1.4 copy-start
  1.5 1.4 copy-start.1

commit v3 on v2

--- a/solution.py
+++ b/solution.py
@@ -142,14 +142,14 @@
 N_COL = 4
 LOG2E = 1.4426950408889634
 KEY, VAL, QUE, OUT = range(4)
-PIECES = ((KEY, 0, 1), (VAL, 0, 1), (QUE, 0, 2), (QUE, 1, 2), (OUT, 0, 2), (OUT, 1, 2))
-K_0, V_0, Q_0, Q_1, O_0, O_1 = range(6)
+PIECES = ((KEY, 0, 1), (VAL, 0, 1), (QUE, 0, 2), (QUE, 1, 2), (OUT, 0, 4), (OUT, 1, 4), (OUT, 2, 4), (OUT, 3, 4))
+K_0, V_0, Q_0, Q_1, O_0, O_1, O_2, O_3 = range(8)
 
 
 def block_kernel(
     tok, gain, kw, vw, qw, ow, cosine, sine, first,
     out,
-    x_all, normed, wk, wv, wq, wo, keys, values, queries, mixed,
+    x_all, normed, wk, wv, wq, wo, keys, values, queries, mixed, total,
     z_send, z_recv, y_send, y_recv, t_send, t_recv, l_sem, k_send, k_recv, a_send, a_recv,
 ):
     g = lax.axis_index("grp")
@@ -303,7 +303,7 @@
         scale = lax.rsqrt(total / (N_COL * feats) + 1e-06)
         for b in range(N_COL):
             f = x_all[b, at, :].astype(jnp.float32)
-            normed[b, at, :] = (f * scale * gain[b]).astype(jnp.bfloat16)
+            normed[b, at, :] = (f * scale * gain[b * feats:(b + 1) * feats]).astype(jnp.bfloat16)
         return carry
 
     lax.fori_loop(0, rows // step, norm_rows, 0)
@@ -342,11 +342,11 @@
                 kv_copy(which, d).start()
 
     pass_on((Q_1,), 2)
-    begin((O_0,))
+    begin((O_0, O_1))
     pass_on((Q_0,), 3)
-    begin((O_1,))
+    begin((O_2, O_3))
     pass_on((Q_1,), 3)
-    pass_on((O_0,), 1)
+    pass_on((O_0, O_1), 1)
     arrived((Q_0, Q_1))
 
     def q_rows(t, carry):
@@ -356,7 +356,7 @@
         return carry
 
     lax.fori_loop(0, rows // tile, q_rows, 0)
-    pass_on((O_1,), 1)
+    pass_on((O_2, O_3), 1)
     for d in (1, 2):
         @pl.when(s >= d)
         def _():
@@ -414,30 +414,53 @@
 
     attend_rows(0, 0, tiles)
     share(0)
-    pass_on((O_0,), 2)
+    pass_on((O_0, O_1), 2)
     attend_rows(1, 0, tiles // 2)
-    pass_on((O_1,), 2)
+    pass_on((O_2, O_3), 2)
     attend_rows(1, tiles // 2, tiles)
     share(1)
     mixed_on(0)
     mixed_on(1)
-    pass_on((O_0,), 3)
-    pass_on((O_1,), 3)
-
     for e in range(kv_local):
         mixed_copy(1, e, core).wait_recv()
         mixed_copy(2, e, far).wait_recv()
-    arrived((O_0, O_1))
+    width = 384
+
+    def add_rows(b):
+        def body(t, carry):
+            at = pl.ds(pl.multiple_of(t * tile, tile), tile)
+            for lo in range(0, feats, width):
+                cols = slice(lo, lo + width)
+                total[at, cols] = total[at, cols] + jnp.dot(
+                    mixed[b, at, :], wo[b, :, cols], preferred_element_type=jnp.float32)
+            return carry
+
+        lax.fori_loop(0, rows // tile, body, 0)
+
+    def start_rows(t, carry):
+        at = pl.ds(pl.multiple_of(t * tile, tile), tile)
+        for lo in range(0, feats, width):
+            cols = slice(lo, lo + width)
+            total[at, cols] = x_all[c, at, cols].astype(jnp.float32) + jnp.dot(
+                mixed[s, at, :], wo[s, :, cols], preferred_element_type=jnp.float32)
+        return carry
+
+    lax.fori_loop(0, rows // tile, start_rows, 0)
+    o_all = (O_0, O_1, O_2, O_3)
+    for r in range(1, N_SEQ):
+        if r == N_SEQ - 1:
+            for p in o_all:
+                pass_on((p,), r)
+        for d in range(2):
+            @pl.when(came(d, r))
+            def _():
+                for p in o_all:
+                    y_copy(p, d, r, 1 - g).wait_recv()
+                add_rows(s - signs[d] * r)
 
     def out_rows(t, carry):
         at = pl.ds(pl.multiple_of(t * tile, tile), tile)
-        for lo in range(0, feats, 384):
-            cols = slice(lo, lo + 384)
-            total = jnp.dot(mixed[0, at, :], wo[0, :, cols], preferred_element_type=jnp.float32)
-            for b in range(1, N_COL):
-                total = total + jnp.dot(
-                    mixed[b, at, :], wo[b, :, cols], preferred_element_type=jnp.float32)
-            out[at, cols] = (x_all[c, at, cols].astype(jnp.float32) + total).astype(jnp.bfloat16)
+        out[at, :] = total[at, :].astype(jnp.bfloat16)
         return carry
 
     lax.fori_loop(0, rows // tile, out_rows, 0)
@@ -474,7 +497,6 @@
     sine = jnp.concatenate([-sine, sine], axis=1)
     index = lax.axis_index("seq") * rows + jnp.arange(rows, dtype=jnp.int32)
     first = (index - positions)[:, None]
-    gain = norm_gain.reshape(N_COL, 1, feats)
     bf16 = jnp.bfloat16
     dma = pltpu.SemaphoreType.DMA
     anywhere = pl.BlockSpec(memory_space=pl.ANY)
@@ -497,12 +519,13 @@
             pltpu.VMEM((3, rows, kv_cols), bf16),
             pltpu.VMEM((rows, q_cols), bf16),
             pltpu.VMEM((N_COL, rows, q_cols), bf16),
-            dma((6, 2, 3)), dma((6, 2, 3)), dma((6, 2, 3)), dma((6, 2, 3)),
+            pltpu.VMEM((rows, feats), jnp.float32),
+            dma((8, 2, 3)), dma((8, 2, 3)), dma((8, 2, 3)), dma((8, 2, 3)),
             dma((3,)), dma((3,)), dma((5,)), dma((2, 2)), dma((2, 2)), dma((3, 2)), dma((3, 2)),
         ],
         compiler_params=pltpu.CompilerParams(
             collective_id=0, has_side_effects=True, vmem_limit_bytes=52 * 1024 * 1024),
-    )(tokens, gain, key_weight, value_weight, query_weight, out_weight, cosine, sine, first)
+    )(tokens, norm_gain, key_weight, value_weight, query_weight, out_weight, cosine, sine, first)
 
 
 def solution(mesh):

time: 160 us -> 163 us (1.019); the launches traced: 157 us -> 162 us
  Pallas kernels: 152 us -> 158 us
    pallas_call x1, Pallas kernels: 152 us -> 158 us  [fused_device(): pl.pallas_call(block_kernel, out_shape=jax.ShapeDtypeStruct((rows, feats)...]
where the time goes in v3:
time: 163 us; the launch traced here: 162 us
  Pallas kernels  158 us (97%)
  local copies, waits for them, and re-layouts  2.53 us (2%)
  other arithmetic  1.97 us (1%)
    pallas_call x1, Pallas kernels, fused_device(): pl.pallas_call(block_kernel, out_shape=jax.ShapeDtypeStruct((rows, feats)...  158 us

profile of v3, /device:TPU:31, one launch (start us, length us, event | category | flops | bytes accessed | tf_op | source)
XLA Modules:
  0.0 162.3 jit_solution(15665049723347301388)
XLA Ops:
  0.0 0.8 add_subtract_fusion
  0.8 0.0 copy-start
  0.8 0.0 copy-start.1
  0.8 0.0 copy-start.2
  0.8 0.1 copy.8.first
  0.9 1.0 fusion
  1.9 0.2 pad_maximum_fusion
  2.2 0.0 copy-done
  2.2 0.0 copy-done.1
  2.2 0.0 copy-done.2
  2.2 157.7 %shard_map.73 = bf16[512,1152]{1,0:T(8,128)(2,1)} custom-call(bf16[512,1152]{1,0:T(8,128)(2,1)} %tok.1, f32[4608]{0:T(1024)S(1)} %copy-done.2, bf16[1152,256]{1,0:T(8,128)(2,1)S(1)} %copy-done, bf16[1152,256]{1,0:T(8,128)(2,1)S(1)} %copy-done.1, bf16[1152,512]{1,0:T(8,128)(2,1)} %qw.1, bf16[512,1152]{1,0:T(8,128)(2,1)} %ow.1, ...), custom_call_target="tpu_custom_call" | custom-call | tf_op jit(solution)/shard_map/pallas_call | solution.py:506
  159.9 2.4 %copy.10 = bf16[512,1152]{1,0:T(8,128)(2,1)} copy(bf16[512,1152]{1,0:T(8,128)(2,1)} %shard_map.73) | data formatting | bytes 2359296
  (1 shorter events, 0.0 us)
Async XLA Ops:
  0.8 1.4 copy-start
  0.8 1.4 copy-start.1
  0.8 1.4 copy-start.2
